TPU v7x, 32 devices: a whole 2x2x4 slice. The times are simulated.
32 devices in a mesh: pipe: 2 (over y), ctx: 4 (over z), dp: 4 (over x, core).
Axes of the slice: x: 2, y: 2, z: 4, core: 2. Of those that a mesh axis runs over, the one named last changes fastest.
Arguments:
- state: bfloat16 [2, 4, 512, 1024], P('pipe', 'dp', 'ctx'), may hold values from -36 to 36
- weights: bfloat16 [2, 2, 1024, 256], P(None, 'pipe'), may hold values from -0.1875 to 0.1875
- out_grad: bfloat16 [2, 2, 4, 512, 1024], P(None, 'pipe', 'dp', 'ctx'), may hold values from -0.59765625 to 0.59765625
- start_span: int32 [2, 4], P(None, 'dp'), may hold values from 0 to 1
- block_order: int32 [8], replicated, may hold values from 0 to 7, each once
Outputs:
- state_out: bfloat16 [2, 4, 512, 1024], P('pipe', 'dp', 'ctx')
- weight_grads: float32 [2, 2, 1024, 256], P(None, 'pipe')
All inputs are finite; a program needn't handle non-finite values.
Results may differ from a plain program's by a relative error of at most 0.012.
Values may be sent and summed in bfloat16 or wider, within the bound.
A program may use at most 64 MiB of HBM per device.

v0:
```python
import math

import jax
import jax.numpy as jnp
from jax import lax
from jax.sharding import PartitionSpec as P

EPS = 1e-05


def from_behind(block, axis, distance):
    devices = range(lax.axis_size(axis))
    route = [((i - distance) % len(devices), i) for i in devices]
    return lax.ppermute(block, axis, route)


def rms_scale(values):
    return lax.rsqrt(jnp.mean(values * values, axis=-1, keepdims=True) + EPS)


def token_positions(block_order, seq_total):
    half_count = block_order.shape[0]
    half_len = seq_total // half_count
    row_ids = jnp.arange(seq_total, dtype=jnp.int32)
    selected = (row_ids // half_len)[:, None] == jnp.arange(half_count, dtype=jnp.int32)[None, :]
    block_ids = jnp.sum(jnp.where(selected, block_order[None, :], 0), axis=1)
    return block_ids * half_len + row_ids % half_len


def shards(state, weights, out_grad, start_span, block_order):
    tok_rows = state.shape[2]
    feat_width = state.shape[3]
    head_dim = weights.shape[3] // 2
    head_count = feat_width // head_dim
    group_size = math.gcd(head_count, 4)
    group_count = head_count // group_size
    span_count = weights.shape[0]
    section_count = lax.axis_size("pipe")
    seq_total = tok_rows * lax.axis_size("ctx")
    score_scale = 1.0 / math.sqrt(head_dim)
    all_positions = token_positions(block_order, seq_total)
    own_positions = lax.dynamic_slice_in_dim(
        all_positions, lax.axis_index("ctx") * tok_rows, tok_rows
    )
    causal = all_positions[None, :] <= own_positions[:, None]
    section_index = lax.axis_index("pipe")
    carried = state[0, 0]
    start_column = start_span[:, 0]
    weight_grads = jnp.zeros((span_count, feat_width, 2 * head_dim), jnp.float32)
    for tick_index in range(out_grad.shape[0]):
        anchor = (section_index - tick_index) % section_count
        first_span = jnp.sum(
            jnp.where(jnp.arange(section_count, dtype=jnp.int32) == anchor, start_column, 0)
        )
        span_index = (first_span + (anchor + tick_index) // section_count) % 2
        weight = lax.dynamic_index_in_dim(weights[:, 0], span_index, 0, keepdims=False)
        widened = carried.astype(jnp.float32)
        normed = (widened * rms_scale(widened)).astype(jnp.bfloat16)
        split_heads = widened.reshape(tok_rows, head_count, head_dim)
        queries = (split_heads * rms_scale(split_heads)).astype(jnp.bfloat16)
        projected = jnp.dot(normed, weight, preferred_element_type=jnp.float32)
        key_raw = projected[:, :head_dim]
        key_scale = rms_scale(key_raw)
        key_unit = key_raw * key_scale
        own_rows = jnp.concatenate([key_unit, projected[:, head_dim:]], axis=1).astype(jnp.bfloat16)
        gathered = lax.all_gather(own_rows, "ctx", axis=0, tiled=True)
        key_rows = gathered[:, :head_dim]
        value_rows = gathered[:, head_dim:]
        query_groups = queries.reshape(tok_rows, group_count, group_size, head_dim).transpose(
            1, 0, 2, 3
        )

        def forward_group(query_part):
            scores = (
                jnp.einsum("qhd,kd->hqk", query_part, key_rows, preferred_element_type=jnp.float32)
                * score_scale
            )
            exponent = jnp.where(causal[None], jnp.exp(scores), 0.0)
            total_weight = jnp.sum(exponent, axis=-1, keepdims=True)
            probs = (exponent / total_weight).astype(jnp.bfloat16)
            attended = jnp.einsum(
                "hqk,kd->qhd", probs, value_rows, preferred_element_type=jnp.float32
            )
            return (probs, attended)

        probs, attended = lax.map(forward_group, query_groups)
        output = attended.transpose(1, 0, 2, 3).reshape(tok_rows, feat_width)
        updated = (widened + output * rms_scale(output)).astype(jnp.bfloat16)
        carried = from_behind(updated, "pipe", 1)
        upstream = out_grad[tick_index, 0, 0]
        upstream_groups = upstream.reshape(tok_rows, group_count, group_size, head_dim).transpose(
            1, 0, 2, 3
        )
        row_delta = jnp.sum(upstream_groups.astype(jnp.float32) * attended, axis=-1).transpose(
            0, 2, 1
        )
        key_grad = jnp.zeros((tok_rows * lax.axis_size("ctx"), head_dim), jnp.float32)
        value_grad = jnp.zeros((tok_rows * lax.axis_size("ctx"), head_dim), jnp.float32)
        for head_block in range(group_count):
            prob_part = probs[head_block]
            value_grad = value_grad + jnp.einsum(
                "hqk,qhd->kd",
                prob_part,
                upstream_groups[head_block],
                preferred_element_type=jnp.float32,
            )
            prob_grad = jnp.einsum(
                "qhd,kd->hqk",
                upstream_groups[head_block],
                value_rows,
                preferred_element_type=jnp.float32,
            )
            score_grad = (
                prob_part.astype(jnp.float32)
                * (prob_grad - row_delta[head_block][..., None])
                * score_scale
            ).astype(jnp.bfloat16)
            key_grad = key_grad + jnp.einsum(
                "hqk,qhd->kd",
                score_grad,
                query_groups[head_block],
                preferred_element_type=jnp.float32,
            )
        key_sums = lax.psum_scatter(
            jnp.concatenate([key_grad, value_grad], axis=1).astype(jnp.bfloat16),
            "ctx",
            scatter_dimension=0,
            tiled=True,
        ).astype(jnp.float32)
        key_delta = key_sums[:, :head_dim]
        key_back = key_scale * (
            key_delta - key_unit * jnp.mean(key_delta * key_unit, axis=-1, keepdims=True)
        )
        grad_rows = jnp.concatenate([key_back, key_sums[:, head_dim:]], axis=1).astype(jnp.bfloat16)
        local_grad = lax.dot_general(
            normed, grad_rows, (((0,), (0,)), ((), ())), preferred_element_type=jnp.float32
        )
        span_mask = (jnp.arange(span_count, dtype=jnp.int32) == span_index).astype(jnp.float32)[
            :, None, None
        ]
        masked_grad = span_mask * local_grad
        weight_grads = weight_grads + masked_grad
    weight_grads = lax.psum(weight_grads, ("ctx", "dp"))
    return (carried[None, None], weight_grads[:, None])


def solution(mesh):
    return jax.shard_map(
        shards,
        mesh=mesh,
        in_specs=(
            P("pipe", "dp", "ctx", None),
            P(None, "pipe", None, None),
            P(None, "pipe", "dp", "ctx", None),
            P(None, "dp"),
            P(),
        ),
        out_specs=(P("pipe", "dp", "ctx", None), P(None, "pipe", None, None)),
        check_vma=False,
    )
```

profile of v0, /device:TPU:17, one launch (start us, length us, event | category | flops | bytes accessed | tf_op | source)
XLA Modules:
  0.0 226.2 jit_solution(1434660903935521940)
XLA Ops:
  7.3 1.4 fusion.193
  9.4 1.1 fusion.132
  10.5 1.2 fusion.128
  11.9 1.0 fusion.130
  13.2 10.7 %all_gather.6 = bf16[512,256]{1,0:T(8,128)(2,1)S(1)} all-gather(bf16[128,256]{1,0:T(8,128)(2,1)S(1)} %pad_maximum_fusion.2), channel_id=1, replica_groups=mesh['pipe'=2,'ctx'=4,'dp'=4] {'ctx'}, dimensions={0}, use_global_device_ids=true | all-gather | bytes 327680 | tf_op jit(solution)/shard_map/all_gather | solution.py:66
  23.9 0.7 fusion.212
  25.2 1.1 broadcast.232.clone2
  26.3 8.9 %while.26 = (s32[]{:T(128)}, bf16[2,4,128,512]{2,3,1,0:T(8,128)(2,1)}, f32[2,128,4,128]{3,1,2,0:T(8,128)S(1)}, bf16[2,128,4,128]{1,3,2,0:T(8,128)(2,1)S(1)}, bf1...) while((s32[]{:T(128)}, ...), condition=%wide.region_7.8_spmd.clone, body=%wide.region_5.7_spmd.clone.sunk | while | flops 203491328 | bytes 3739245 | solution.py:86
  26.4 1.8 fusion.233
  28.2 1.4 fusion.232
  29.6 0.3 copy.225
  29.9 0.8 constant_dynamic-update-slice_fusion.4
  30.9 1.8 fusion.233
  32.7 1.4 fusion.232
  34.4 0.8 constant_dynamic-update-slice_fusion.4
  35.4 0.3 copy.152
  35.7 1.0 reshape.174
  36.7 2.0 fusion.133
  38.7 1.2 collective-permute-start
  39.9 1.8 fusion.210
  41.7 0.8 copy.219
  42.5 1.1 copy.159
  43.9 1.0 convolution_bitcast_fusion.8
  44.9 2.2 fusion.104
  47.1 2.2 fusion.113
  49.2 1.2 fusion.111
  50.5 1.6 pad_maximum_fusion
  53.2 0.5 compare_convert_fusion
  53.9 0.3 fusion.126
  54.4 12.5 %all_gather.7 = bf16[512,256]{1,0:T(8,128)(2,1)S(1)} all-gather(bf16[128,256]{1,0:T(8,128)(2,1)S(1)} %pad_maximum_fusion.3), channel_id=1, replica_groups=mesh['pipe'=2,'ctx'=4,'dp'=4] {'ctx'}, dimensions={0}, use_global_device_ids=true | all-gather | bytes 327680 | tf_op jit(solution)/shard_map/all_gather | solution.py:66
  66.9 0.8 fusion.211
  68.3 0.8 fusion.154
  69.0 1.1 broadcast.232.clone
  70.2 9.2 %while.27 = (s32[]{:T(128)}, bf16[2,4,128,512]{2,3,1,0:T(8,128)(2,1)}, f32[2,128,4,128]{3,1,2,0:T(8,128)S(1)}, bf16[2,128,4,128]{1,3,2,0:T(8,128)(2,1)}, bf16[51...) while((s32[]{:T(128)}, ...), condition=%wide.region_15.16_spmd.clone, body=%wide.region_13.15_spmd.clone.sunk | while | flops 203491328 | bytes 3739245 | solution.py:86
  70.3 1.9 fusion.240
  72.1 1.5 fusion.239
  73.6 0.3 copy.226
  73.9 0.8 constant_dynamic-update-slice_fusion.5
  74.8 1.9 fusion.240
  76.7 1.5 fusion.239
  78.2 0.3 copy.226
  78.5 0.8 constant_dynamic-update-slice_fusion.5
  79.5 0.6 slice_bitcast_fusion.25
  80.1 1.3 convolution_bitcast_fusion.6
  81.4 2.0 fusion.110
  83.4 2.2 fusion.102
  85.6 2.2 fusion.112
  87.8 1.7 pad_maximum_fusion.1
  89.7 0.9 fusion.170
  90.6 0.8 slice.151
  91.4 0.9 fusion.172
  92.3 0.4 fusion.155
  92.6 20.8 %reduce-scatter.5.cloned.1.call-done = bf16[128,256]{1,0:T(8,128)(2,1)} async-done(((bf16[512,256]{1,0:T(8,128)(2,1)}), bf16[128,256]{1,0:T(8,128)(2,1)}) %reduce-scatter.5.cloned.1.call-update) | async-done | bytes 65552 | tf_op jit(solution)/shard_map/reduce_scatter | solution.py:124
  113.5 0.9 fusion.173
  114.4 0.8 slice.159
  115.2 0.9 fusion.175
  116.0 0.4 fusion.169
  116.5 1.7 add_bitcast_fusion
  118.1 0.3 copy.156
  119.0 1.3 collective-permute-start.1
  120.3 4.4 %collective-permute-done.1 = bf16[128,1024]{1,0:T(8,128)(2,1)S(1)} collective-permute-done((bf16[128,1024]{1,0:T(8,128)(2,1)S(1)}, bf16[128,1024]{1,0:T(8,128)(2,1)S(1)}, u32[]{:S(2)}, u32[]{:S(2)}) %collective-permute-start.1) | collective-permute-done | bytes 262176 | tf_op jit(solution)/shard_map/ppermute | solution.py:14
  124.7 91.3 %all-reduce.2.cloned.1.call-done = f32[2,1,1024,256]{3,2,1,0:T(8,128)} async-done(((f32[2,1,1024,256]{3,2,1,0:T(8,128)}), f32[2,1,1024,256]{3,2,1,0:T(8,128)}) %all-reduce.2.cloned.1.call-update) | async-done | bytes 2097168 | tf_op jit(solution)/shard_map/psum | solution.py:143
  216.0 0.7 copy.255
  216.7 3.0 %copy.256 = f32[2,1,1024,256]{3,2,1,0:T(8,128)} copy(f32[2,1,1024,256]{3,2,1,0:T(8,128)} %all-reduce.2.cloned.1.call-done) | data formatting | bytes 4194304
  (92 shorter events, 4.3 us)
Async XLA Ops:
  7.2 3.3 %copy-start = (bf16[2,1,1024,256]{3,2,1,0:T(8,128)(2,1)S(1)}, bf16[2,1,1024,256]{3,2,1,0:T(8,128)(2,1)}, u32[]{:S(2)}) copy-start(bf16[2,1,1024,256]{3,2,1,0:T(8,128)(2,1)} %param.10) | copy-start | bytes 3145732
  7.2 5.7 %copy-start.1 = (bf16[1,1,128,1024]{3,2,1,0:T(8,128)(2,1)S(1)}, bf16[1,1,128,1024]{3,2,1,0:T(8,128)(2,1)}, u32[]{:S(2)}) copy-start(bf16[1,1,128,1024]{3,2,1,0:T(8,128)(2,1)} %param.9) | copy-start | bytes 786436
  7.2 5.8 %copy-start.17 = (s32[8]{0:T(128)S(1)}, s32[8]{0:T(128)}, u32[]{:S(2)}) copy-start(s32[8]{0:T(128)} %param.13) | copy-start | bytes 100
  7.2 82.5 %reduce-scatter.3.cloned.1.call-start = ((), (), s32[]{:S(2)}) async-start(), calls=%async_computation.2 | async-start | bytes 327680 | tf_op jit(solution)/shard_map/reduce_scatter | solution.py:124
  10.5 2.5 %copy-start.11 = (f32[128]{0:T(128)}, f32[128]{0:T(128)S(1)}, u32[]{:S(2)}) copy-start(f32[128]{0:T(128)S(1)} %add_rsqrt_fusion.7) | copy-start | bytes 1540
  23.9 2.4 %copy-start.6 = (bf16[512,256]{1,0:T(8,128)(2,1)}, bf16[512,256]{1,0:T(8,128)(2,1)S(1)}, u32[]{:S(2)}) copy-start(bf16[512,256]{1,0:T(8,128)(2,1)S(1)} %all_gather.6) | copy-start | bytes 786436
  35.2 3.5 %copy-start.10 = (bf16[2,128,4,128]{1,3,2,0:T(8,128)(2,1)}, bf16[2,128,4,128]{1,3,2,0:T(8,128)(2,1)S(1)}, u32[]{:S(2)}) copy-start(bf16[2,128,4,128]{1,3,2,0:T(8,128)(2,1)S(1)} %get-tuple-element.433) | copy-start | bytes 786436
  36.7 7.2 %copy-start.3 = (bf16[2,4,128,512]{2,3,1,0:T(8,128)(2,1)S(1)}, bf16[2,4,128,512]{2,3,1,0:T(8,128)(2,1)}, u32[]{:S(2)}) copy-start(bf16[2,4,128,512]{2,3,1,0:T(8,128)(2,1)} %get-tuple-element.80) | copy-start | bytes 3145732
  38.7 15.1 %collective-permute-start = (bf16[128,1024]{1,0:T(8,128)(2,1)}, bf16[128,1024]{1,0:T(8,128)(2,1)S(1)}, u32[]{:S(2)}, u32[]{:S(2)}) collective-permute-start(bf16[128,1024]{1,0:T(8,128)(2,1)} %fusion.133), channel_id=1, source_target_pairs={{16,0},{0,16},{17,1},{1,17},{18,2},{2,18},{19,3},{3,19},{20,4},{4,... | collective-permute-start | bytes 786440 | tf_op jit(solution)/shard_map/ppermute | solution.py:14
  43.8 3.2 %copy-start.7 = (bf16[512,256]{1,0:T(8,128)(2,1)S(1)}, bf16[512,256]{1,0:T(8,128)(2,1)}, u32[]{:S(2)}) copy-start(bf16[512,256]{1,0:T(8,128)(2,1)} %copy-done.6) | copy-start | bytes 786436
  47.1 5.8 %copy-start.9 = (bf16[1,1,1,128,1024]{4,3,2,1,0:T(8,128)(2,1)S(1)}, bf16[1,1,1,128,1024]{4,3,2,1,0:T(8,128)(2,1)}, u32[]{:S(2)}) copy-start(bf16[1,1,1,128,1024]{4,3,2,1,0:T(8,128)(2,1)} %get-tuple-element.253) | copy-start | bytes 786436
  52.1 61.3 %reduce-scatter.5.cloned.1.call-start = ((), (), s32[]{:S(2)}) async-start(), calls=%async_computation.3 | async-start | bytes 327680 | tf_op jit(solution)/shard_map/reduce_scatter | solution.py:124
  53.9 13.9 %copy-start.13 = (f32[128]{0:T(128)}, f32[128]{0:T(128)S(1)}, u32[]{:S(2)}) copy-start(f32[128]{0:T(128)S(1)} %add_rsqrt_fusion.4) | copy-start | bytes 1540
  54.2 13.6 %copy-start.4 = (f32[128,256]{1,0:T(8,128)}, f32[128,256]{1,0:T(8,128)S(1)}, u32[]{:S(2)}) copy-start(f32[128,256]{1,0:T(8,128)S(1)} %fusion.126) | copy-start | bytes 393220
  66.9 0.8 copy-start.8
  79.3 4.1 %copy-start.2 = (bf16[2,4,128,512]{2,3,1,0:T(8,128)(2,1)S(1)}, bf16[2,4,128,512]{2,3,1,0:T(8,128)(2,1)}, u32[]{:S(2)}) copy-start(bf16[2,4,128,512]{2,3,1,0:T(8,128)(2,1)} %get-tuple-element.81) | copy-start | bytes 3145732
  83.4 8.8 %copy-start.12 = (f32[128]{0:T(128)S(1)}, f32[128]{0:T(128)}, u32[]{:S(2)}) copy-start(f32[128]{0:T(128)} %copy-done.11) | copy-start | bytes 1540
  85.6 30.4 %copy-start.14 = (f32[128]{0:T(128)S(1)}, f32[128]{0:T(128)}, u32[]{:S(2)}) copy-start(f32[128]{0:T(128)} %copy-done.13) | copy-start | bytes 1540
  87.8 25.6 %copy-start.5 = (f32[128,256]{1,0:T(8,128)S(1)}, f32[128,256]{1,0:T(8,128)}, u32[]{:S(2)}) copy-start(f32[128,256]{1,0:T(8,128)} %copy-done.4) | copy-start | bytes 393220
  87.8 28.6 %copy-start.15 = (f32[2]{0:T(128)S(1)}, f32[2]{0:T(128)}, u32[]{:S(2)}) copy-start(f32[2]{0:T(128)} %get-tuple-element.264) | copy-start | bytes 28
  87.8 28.6 %copy-start.16 = (f32[2]{0:T(128)S(1)}, f32[2]{0:T(128)}, u32[]{:S(2)}) copy-start(f32[2]{0:T(128)} %get-tuple-element.265) | copy-start | bytes 28
  89.6 126.4 %all-reduce.2.cloned.1.call-start = ((), (), s32[]{:S(2)}) async-start(), calls=%async_computation.4 | async-start | bytes 4194304 | tf_op jit(solution)/shard_map/psum | solution.py:143
  119.0 5.7 %collective-permute-start.1 = (bf16[128,1024]{1,0:T(8,128)(2,1)S(1)}, bf16[128,1024]{1,0:T(8,128)(2,1)S(1)}, u32[]{:S(2)}, u32[]{:S(2)}) collective-permute-start(bf16[128,1024]{1,0:T(8,128)(2,1)S(1)} %add_convert_fusion), channel_id=1, source_target_pairs={{16,0},{0,16},{17,1},{1,17},{18,2},{2,18},{19,3},{3,19},{20,4},{4,... | collective-permute-start | bytes 786440 | tf_op jit(solution)/shard_map/ppermute | solution.py:14
Sparse Core Ops, SparseCore 0:
  52.3 21.7 reduce-scatter.2
  89.7 23.7 reduce-scatter.4
  118.3 97.6 all-reduce.1
where the time goes:
time: 231 us; the launch traced here: 226 us
  waiting for transfers between devices  117 us (51%)
  matrix products  29.7 us (13%)
  blocking collectives  23.1 us (10%)
  local copies, waits for them, and re-layouts  20.8 us (9%)
  other arithmetic  17.7 us (8%)
  between operations  15.6 us (7%)
  starting transfers between devices  2.62 us (1%)
    psum x1, waiting for transfers between devices, shards(): weight_grads = lax.psum(weight_grads, ('ctx', 'dp'))  91.3 us
    all_gather x2, blocking collectives, shards(): gathered = lax.all_gather(own_rows, 'ctx', axis=0, tiled=True)  23.1 us
    reduce_scatter x2, waiting for transfers between devices, shards(): lax.psum_scatter(jnp.concatenate([key_grad, value_grad], axis=1).astype(j...  20.8 us
    dot_general x4, matrix products, shards(): jnp.einsum('hqk,qhd->kd', score_grad, query_groups[head_block], preferred...  8.76 us
    dot_general x4, matrix products, forward_group(): jnp.einsum('hqk,kd->qhd', probs, value_rows, preferred_element_type=jnp.f...  7.3 us
    div x4, matrix products, forward_group(): probs = (exponent / total_weight).astype(jnp.bfloat16)  5.79 us
    dot_general x4, matrix products, shards(): jnp.einsum('hqk,qhd->kd', prob_part, upstream_groups[head_block], preferr...  5.54 us
    unnamed x42, local copies, waits for them, and re-layouts  5.03 us
  transfers between devices with their start and end apart: 5, of which 3 were waited for; matrix products, arithmetic and copies ran while one was open for 18% of the time, Pallas kernels for 0%

commit v1 on v0

v1 whole, which is shorter than its diff:
```python
import functools
import math

import jax
import jax.numpy as jnp
from jax import lax
from jax.experimental import pallas as pl
from jax.experimental.pallas import tpu as pltpu
from jax.sharding import PartitionSpec as P

EPS = 1e-05
F32 = jnp.float32
BF16 = jnp.bfloat16
MESH = pl.DeviceIdType.MESH


def dot(a, b):
    return jnp.dot(a, b, preferred_element_type=F32)


def dot_nt(a, b):
    return lax.dot_general(a, b, (((1,), (1,)), ((), ())), preferred_element_type=F32)


def steps(count, body):
    if count <= 4:
        for index in range(count):
            body(index)
    else:
        lax.fori_loop(0, count, lambda index, none: (body(index), none)[1], None)


def kernel(
    cfg,
    state_ref,
    weights_ref,
    upstream_ref,
    span_ref,
    order_ref,
    state_out,
    gathered,
    kv,
    queries,
    up_rows,
    up_cols,
    exps,
    out_cols,
    totals,
    deltas,
    key_raw,
    updated,
    arrived,
    normed_t,
    normed_in,
    terms_out,
    terms_in,
    term_own,
    grad_rows,
    slices,
    wsend,
    wrecv,
    kv_send,
    kv_recv,
    nt_send,
    nt_recv,
    kt_send,
    kt_recv,
    gr_send,
    gr_recv,
    st_send,
    st_recv,
    ws_send,
    ws_recv,
    ga_send,
    ga_recv,
    gb_send,
    gb_recv,
):
    n_pipe, n_ctx, n_dp, ticks, half_len = cfg
    rows, feat = state_ref.shape
    hd = weights_ref.shape[2] // 2
    heads = feat // hd
    stack = heads * rows
    width = min(stack, 2 * rows)
    chunks = [slice(i * width, (i + 1) * width) for i in range(stack // width)]
    per_dev = rows // half_len
    f_ctx = feat // n_ctx
    f_dp = f_ctx // n_dp
    score_scale = 1.0 / math.sqrt(hd)
    exp_scale = score_scale * math.log2(math.e)

    sec = lax.axis_index("pipe")
    me = lax.axis_index("ctx")
    lane = lax.axis_index("dp")
    behind = lax.rem(sec + n_pipe - 1, n_pipe)
    ahead = lax.rem(sec + 1, n_pipe)

    def ctx_peer(offset):
        return lax.rem(me + offset, n_ctx)

    def dp_peer(offset):
        return lax.rem(lane + offset, n_dp)

    barrier = pltpu.get_barrier_semaphore()

    def greet(axis, who):
        pl.semaphore_signal(barrier, inc=1, device_id={axis: who}, device_id_type=MESH)

    for o in range(1, n_ctx):
        greet("ctx", ctx_peer(o))
    for o in range(1, n_dp):
        greet("dp", dp_peer(o))
    greet("pipe", behind)
    greet("pipe", ahead)

    def remote(src, dst, send, recv, axis, who):
        return pltpu.make_async_remote_copy(
            src_ref=src,
            dst_ref=dst,
            send_sem=send,
            recv_sem=recv,
            device_id={axis: who},
            device_id_type=MESH,
        )

    def kv_copy(t, o, owner, to):
        return remote(
            kv.at[t, owner], kv.at[t, owner], kv_send.at[t, o], kv_recv.at[t, owner], "ctx", to
        )

    def nt_copy(t, o, frm, to):
        return remote(
            normed_t.at[t, pl.ds(pl.multiple_of(to * f_ctx, 16), f_ctx)],
            normed_in.at[t, frm],
            nt_send.at[t, o],
            nt_recv.at[t, frm],
            "ctx",
            to,
        )

    def kt_copy(t, o, frm, to):
        return remote(
            terms_out.at[t, to],
            terms_in.at[t, frm],
            kt_send.at[t, o],
            kt_recv.at[t, frm],
            "ctx",
            to,
        )

    def gr_copy(t, o, owner, to):
        return remote(
            grad_rows.at[t, owner],
            grad_rows.at[t, owner],
            gr_send.at[t, o],
            gr_recv.at[t, owner],
            "ctx",
            to,
        )

    def st_copy(t):
        dst = state_out if t == ticks - 1 else arrived.at[t]
        return remote(updated.at[t], dst, st_send.at[t], st_recv.at[t], "pipe", ahead)

    def ws_copy(o, frm, to):
        return remote(wsend.at[to], wrecv.at[frm], ws_send.at[o], ws_recv.at[frm], "dp", to)

    def ga_copy(o, owner, to):
        return remote(
            gathered.at[owner, lane],
            gathered.at[owner, lane],
            ga_send.at[o],
            ga_recv.at[owner],
            "ctx",
            to,
        )

    def gb_copy(o, c, owner, to):
        return remote(
            gathered.at[c, owner],
            gathered.at[c, owner],
            gb_send.at[o, c],
            gb_recv.at[c, owner],
            "dp",
            to,
        )

    def positions(which, shape, axis):
        row = lax.rem(lax.broadcasted_iota(jnp.int32, shape, axis), rows)
        part = row // half_len
        base = jnp.zeros(shape, jnp.int32)
        for i in range(per_dev):
            base = jnp.where(part == i, order_ref[which * per_dev + i], base)
        return base * half_len + lax.rem(row, half_len)

    own_pos = positions(me, (1, width), 1)

    def span_at(t):
        anchor = lax.rem(sec - t + n_pipe * ticks, n_pipe)
        return lax.rem(span_ref[anchor, 0] + (anchor + t) // n_pipe, 2)

    def begin(t, source):
        x = source[...].astype(F32)
        squares = x * x
        sums = [
            jnp.sum(squares[:, h * hd : (h + 1) * hd], axis=1, keepdims=True) for h in range(heads)
        ]
        scale = lax.rsqrt(sum(sums[1:], sums[0]) * (1.0 / feat) + EPS)
        normed = (x * scale).astype(BF16)
        projected = dot(normed, weights_ref[span_at(t)])
        raw = projected[:, :hd]
        key_raw[t] = raw
        key_unit = raw * lax.rsqrt(jnp.mean(raw * raw, axis=1, keepdims=True) + EPS)
        kv[t, me] = jnp.concatenate([key_unit, projected[:, hd:]], axis=1).astype(BF16)
        if t == 0:
            pl.semaphore_wait(barrier, n_ctx + n_dp)
        for o in range(1, n_ctx):
            kv_copy(t, o, me, ctx_peer(o)).start()
        for h in range(heads):
            part = x[:, h * hd : (h + 1) * hd]
            queries[h * rows : (h + 1) * rows, :] = (
                part * lax.rsqrt(sums[h] * (1.0 / hd) + EPS)
            ).astype(BF16)
            normed_t[t, h * hd : (h + 1) * hd, :] = (part * scale).T.astype(BF16)
            up = upstream_ref[t, :, h * hd : (h + 1) * hd]
            up_rows[h * rows : (h + 1) * rows, :] = up
            up_cols[:, h * rows : (h + 1) * rows] = up.astype(F32).T.astype(BF16)
        for o in range(1, n_ctx):
            nt_copy(t, o, me, ctx_peer(o)).start()

    def attend(t, block, first):
        keys = kv[t, block, :, :hd]
        values_t = kv[t, block, :, hd:].astype(F32).T.astype(BF16)
        causal = positions(block, (rows, 1), 0) <= own_pos
        for cut in chunks:
            scores = dot_nt(keys, queries[cut, :])
            weight = jnp.where(causal, jnp.exp2(scores * exp_scale), 0.0)
            total = jnp.sum(weight, axis=0, keepdims=True)
            rounded = weight.astype(BF16)
            exps[block, :, cut] = rounded
            mixed = dot(values_t, rounded)
            if first:
                totals[:, cut] = total
                out_cols[:, cut] = mixed
            else:
                totals[:, cut] += total
                out_cols[:, cut] += mixed

    def update(t, source):
        inverse = 1.0 / totals[...]
        totals[...] = inverse
        power = jnp.zeros((1, rows), F32)
        for h in range(heads):
            cut = slice(h * rows, (h + 1) * rows)
            part = out_cols[:, cut] * inverse[:, cut]
            out_cols[:, cut] = part
            deltas[:, cut] = jnp.sum(part * up_cols[:, cut].astype(F32), axis=0, keepdims=True)
            power = power + jnp.sum(part * part, axis=0, keepdims=True)
        scale = lax.rsqrt(power * (1.0 / feat) + EPS)
        for h in range(heads):
            cut = slice(h * hd, (h + 1) * hd)
            part = (out_cols[:, h * rows : (h + 1) * rows] * scale).T
            updated[t, :, cut] = (source[:, cut].astype(F32) + part).astype(BF16)
        st_copy(t).start()

    def backward(t, block):
        values = kv[t, block, :, hd:]
        key_grad = jnp.zeros((rows, hd), F32)
        value_grad = jnp.zeros((rows, hd), F32)
        for cut in chunks:
            probs = exps[block, :, cut].astype(F32) * totals[:, cut]
            prob_grad = dot(values, up_cols[:, cut])
            score_grad = (probs * (prob_grad - deltas[:, cut])).astype(BF16)
            value_grad = value_grad + dot(probs.astype(BF16), up_rows[cut, :])
            key_grad = key_grad + dot(score_grad, queries[cut, :])
        return jnp.concatenate([key_grad * score_scale, value_grad], axis=1).astype(BF16)

    def finish_rows(t):
        sums = term_own[t].astype(F32)
        for o in range(1, n_ctx):
            peer = ctx_peer(o)
            kt_copy(t, o, peer, me).wait_recv()
            sums = sums + terms_in[t, peer].astype(F32)
        raw = key_raw[t]
        scale = lax.rsqrt(jnp.mean(raw * raw, axis=1, keepdims=True) + EPS)
        unit = raw * scale
        delta = sums[:, :hd]
        back = scale * (delta - unit * jnp.mean(delta * unit, axis=1, keepdims=True))
        grad_rows[t, me] = jnp.concatenate([back, sums[:, hd:]], axis=1).astype(BF16)
        for o in range(1, n_ctx):
            gr_copy(t, o, me, ctx_peer(o)).start()

    def weight_slice(t):
        own = normed_t[t, pl.ds(pl.multiple_of(me * f_ctx, 16), f_ctx), :]
        total = dot(own, grad_rows[t, me])
        for o in range(1, n_ctx):
            peer = ctx_peer(o)
            nt_copy(t, o, peer, me).wait_recv()
            gr_copy(t, o, peer, me).wait_recv()
            total = total + dot(normed_in[t, peer], grad_rows[t, peer])
        return total

    for t in range(ticks):
        if t == 0:
            source = state_ref
        else:
            st_copy(t - 1).wait_recv()
            source = arrived.at[t - 1]
        begin(t, source)
        attend(t, me, True)
        if t > 0:
            finish_rows(t - 1)

        def later(index, t=t):
            peer = ctx_peer(index + 1)
            kv_copy(t, 0, peer, me).wait_recv()
            attend(t, peer, False)

        steps(n_ctx - 1, later)
        update(t, source)

        def give(index, t=t):
            peer = ctx_peer(index + 1)
            terms_out[t, peer] = backward(t, peer)
            kt_copy(t, index + 1, me, peer).start()

        steps(n_ctx - 1, give)
        term_own[t] = backward(t, me)

    for t in range(ticks - 1):
        slices[t] = weight_slice(t)
    finish_rows(ticks - 1)
    slices[ticks - 1] = weight_slice(ticks - 1)
    picked = [span_at(t).astype(F32) for t in range(ticks)]
    for d in range(n_dp):
        cut = slice(d * f_dp, (d + 1) * f_dp)
        parts = [slices[t, cut, :] for t in range(ticks)]
        high = sum(part * pick for part, pick in zip(parts, picked))
        low = sum(part * (1.0 - pick) for part, pick in zip(parts, picked))
        wsend[d, 0] = low.astype(BF16)
        wsend[d, 1] = high.astype(BF16)
    for o in range(1, n_dp):
        ws_copy(o, lane, dp_peer(o)).start()
    total = wsend[lane].astype(F32)
    for o in range(1, n_dp):
        peer = dp_peer(o)
        ws_copy(o, peer, lane).wait_recv()
        total = total + wrecv[peer].astype(F32)
    gathered[me, lane] = total.astype(BF16)
    for o in range(1, n_ctx):
        ga_copy(o, me, ctx_peer(o)).start()
    for o in range(1, n_dp):
        gb_copy(o, me, lane, dp_peer(o)).start()
    for o in range(1, n_ctx):
        c = ctx_peer(o)
        ga_copy(o, c, me).wait_recv()
        for k in range(1, n_dp):
            gb_copy(k, c, lane, dp_peer(k)).start()
    for k in range(1, n_dp):
        for c in range(n_ctx):
            gb_copy(k, c, dp_peer(k), lane).wait_recv()
    st_copy(ticks - 1).wait_recv()

    for t in range(ticks):
        st_copy(t).wait_send()
        for o in range(1, n_ctx):
            peer = ctx_peer(o)
            kv_copy(t, o, me, peer).wait_send()
            nt_copy(t, o, me, peer).wait_send()
            kt_copy(t, o, me, peer).wait_send()
            gr_copy(t, o, me, peer).wait_send()
    for o in range(1, n_dp):
        ws_copy(o, lane, dp_peer(o)).wait_send()
        for c in range(n_ctx):
            gb_copy(o, c, lane, dp_peer(o)).wait_send()
    for o in range(1, n_ctx):
        ga_copy(o, me, ctx_peer(o)).wait_send()


def shards(sizes, state, weights, out_grad, start_span, block_order):
    n_pipe, n_ctx, n_dp = sizes
    rows, feat = state.shape[2:]
    spans, cols = weights.shape[0], weights.shape[3]
    hd = cols // 2
    stack = (feat // hd) * rows
    ticks = out_grad.shape[0]
    half_len = rows * n_ctx // block_order.shape[0]
    f_ctx = feat // n_ctx
    f_dp = f_ctx // n_dp
    cfg = (n_pipe, n_ctx, n_dp, ticks, half_len)
    dma = pltpu.SemaphoreType.DMA
    vmem = pl.BlockSpec(memory_space=pltpu.VMEM)
    smem = pl.BlockSpec(memory_space=pltpu.SMEM)
    new_state, gathered = pl.pallas_call(
        functools.partial(kernel, cfg),
        out_shape=(
            jax.ShapeDtypeStruct((rows, feat), BF16),
            jax.ShapeDtypeStruct((n_ctx, n_dp, spans, f_dp, cols), BF16),
        ),
        in_specs=[vmem, vmem, vmem, smem, smem],
        out_specs=(vmem, vmem),
        scratch_shapes=[
            pltpu.VMEM((ticks, n_ctx, rows, cols), BF16),
            pltpu.VMEM((stack, hd), BF16),
            pltpu.VMEM((stack, hd), BF16),
            pltpu.VMEM((hd, stack), BF16),
            pltpu.VMEM((n_ctx, rows, stack), BF16),
            pltpu.VMEM((hd, stack), F32),
            pltpu.VMEM((1, stack), F32),
            pltpu.VMEM((1, stack), F32),
            pltpu.VMEM((ticks, rows, hd), F32),
            pltpu.VMEM((ticks, rows, feat), BF16),
            pltpu.VMEM((ticks, rows, feat), BF16),
            pltpu.VMEM((ticks, feat, rows), BF16),
            pltpu.VMEM((ticks, n_ctx, f_ctx, rows), BF16),
            pltpu.VMEM((ticks, n_ctx, rows, cols), BF16),
            pltpu.VMEM((ticks, n_ctx, rows, cols), BF16),
            pltpu.VMEM((ticks, rows, cols), BF16),
            pltpu.VMEM((ticks, n_ctx, rows, cols), BF16),
            pltpu.VMEM((ticks, f_ctx, cols), F32),
            pltpu.VMEM((n_dp, spans, f_dp, cols), BF16),
            pltpu.VMEM((n_dp, spans, f_dp, cols), BF16),
        ]
        + [dma((ticks, n_ctx))] * 8
        + [dma((ticks,))] * 2
        + [dma((n_dp,))] * 2
        + [dma((n_ctx,))] * 2
        + [dma((n_dp, n_ctx)), dma((n_ctx, n_dp))],
        compiler_params=pltpu.CompilerParams(
            collective_id=0, has_side_effects=True, vmem_limit_bytes=48 * 1024 * 1024
        ),
        name="window",
    )(state[0, 0], weights[:, 0], out_grad[:, 0, 0], start_span, block_order)
    grads = gathered.transpose(2, 0, 1, 3, 4).reshape(spans, feat, cols).astype(F32)
    return (new_state[None, None], grads[:, None])


def solution(mesh):
    sizes = (mesh.shape["pipe"], mesh.shape["ctx"], mesh.shape["dp"])
    return jax.shard_map(
        functools.partial(shards, sizes),
        mesh=mesh,
        in_specs=(
            P("pipe", "dp", "ctx", None),
            P(None, "pipe", None, None),
            P(None, "pipe", "dp", "ctx", None),
            P(None, "dp"),
            P(),
        ),
        out_specs=(P("pipe", "dp", "ctx", None), P(None, "pipe", None, None)),
        check_vma=False,
    )
```

time: 231 us -> 81.5 us (0.35); the launches traced: 226 us -> 80.9 us
  waiting for transfers between devices: 117 us -> 0 us
  Pallas kernels: 0 us -> 73.3 us
  matrix products: 29.7 us -> 0 us
  blocking collectives: 23.1 us -> 0 us
  other arithmetic: 17.7 us -> 0.25 us
  between operations: 15.6 us -> 0.65 us
  local copies, waits for them, and re-layouts: 20.8 us -> 6.78 us
  starting transfers between devices: 2.62 us -> 0 us
    psum x1 -> x0, waiting for transfers between devices: 91.3 us -> none  [shards(): weight_grads = lax.psum(weight_grads, ('ctx', 'dp'))]
    pallas_call x0 -> x1, Pallas kernels: none -> 73.3 us  [shards(): pl.pallas_call(functools.partial(kernel, cfg), out_shape=(jax.ShapeDtypeS...]
    dot_general x16 -> x0, matrix products: 23.9 us -> none  [the longest x4 8.76 us: shards(): jnp.einsum('hqk,qhd->kd', score_grad, query_groups[head_block], preferred...]
    all_gather x2 -> x0, blocking collectives: 23.1 us -> none  [shards(): gathered = lax.all_gather(own_rows, 'ctx', axis=0, tiled=True)]
    reduce_scatter x2 -> x0, waiting for transfers between devices: 20.8 us -> none  [shards(): lax.psum_scatter(jnp.concatenate([key_grad, value_grad], axis=1).astype(j...]
    reduce_sum x14 -> x0, other arithmetic: 5.85 us -> none  [the longest x8 2.07 us: rms_scale(): return lax.rsqrt(jnp.mean(values * values, axis=-1, keepdims=True) + EPS)]
    div x4 -> x0, matrix products: 5.79 us -> none  [forward_group(): probs = (exponent / total_weight).astype(jnp.bfloat16)]
    slice x7 -> x0, local copies, waits for them, and re-layouts: 4.8 us -> none  [the longest x1 1.76 us: shards(): upstream = out_grad[tick_index, 0, 0]]
  transfers between devices with their start and end apart: 5 -> 0, of which waited for: 3 -> 0; matrix products, arithmetic and copies ran while one was open for 18% -> 0% of each run, Pallas kernels for 0% -> 0%
where the time goes in v1:
time: 81.5 us; the launch traced here: 80.9 us
  Pallas kernels  73.3 us (90%)
  local copies, waits for them, and re-layouts  6.78 us (8%)
    pallas_call x1, Pallas kernels, shards(): pl.pallas_call(functools.partial(kernel, cfg), out_shape=(jax.ShapeDtypeS...  73.3 us
    unnamed x10, local copies, waits for them, and re-layouts  5.31 us

profile of v1, /device:TPU:17, one launch (start us, length us, event | category | flops | bytes accessed | tf_op | source)
XLA Modules:
  0.0 80.9 jit_solution(17152731513110384156)
XLA Ops:
  0.6 0.7 copy.8.span_ref
  1.4 0.0 copy-start
  1.4 1.2 %copy-done = bf16[2,1,1024,256]{3,2,1,0:T(8,128)(2,1)S(1)} copy-done((bf16[2,1,1024,256]{3,2,1,0:T(8,128)(2,1)S(1)}, bf16[2,1,1024,256]{3,2,1,0:T(8,128)(2,1)}, u32[]{:S(2)}) %copy-start) | copy-done | bytes 1048600
  2.6 0.0 copy-start.1
  2.6 1.0 %copy-done.1 = bf16[2,1,1,128,1024]{4,3,2,1,0:T(8,128)(2,1)S(1)} copy-done((bf16[2,1,1,128,1024]{4,3,2,1,0:T(8,128)(2,1)S(1)}, bf16[2,1,1,128,1024]{4,3,2,1,0:T(8,128)(2,1)}, u32[]{:S(2)}) %copy-start.1) | copy-done | bytes 524312
  3.6 0.0 copy-start.2
  3.6 0.9 %copy-done.2 = bf16[1,1,128,1024]{3,2,1,0:T(8,128)(2,1)S(1)} copy-done((bf16[1,1,128,1024]{3,2,1,0:T(8,128)(2,1)S(1)}, bf16[1,1,128,1024]{3,2,1,0:T(8,128)(2,1)}, u32[]{:S(2)}) %copy-start.2) | copy-done | bytes 262168
  4.6 0.0 copy-start.3
  4.6 0.7 copy-done.3
  5.2 73.3 %window.1 = (bf16[128,1024]{1,0:T(8,128)(2,1)S(1)}, bf16[4,4,2,64,256]{4,3,2,1,0:T(8,128)(2,1)S(1)}) custom-call(bf16[128,1024]{1,0:T(8,128)(2,1)S(1)} %bitcast.12, bf16[2,1024,256]{2,1,0:T(8,128)(2,1)S(1)} %bitcast.9, bf16[2,128,1024]{2,1,0:T(8,128)(2,1)S(1)} %bitcast.10, s32[2,1]{1,0:T(2,128)S(1)} %copy.8.span_ref, s32[8]{0:T(128)S(1)} %copy-done.3), custom_call_target="tpu_custom_call" | custom-call | tf_op jit(solution)/shard_map/window/pallas_call | solution.py:394
  78.5 0.2 convert_bitcast_fusion
  78.8 1.5 %copy.9 = f32[2,4,4,64,256]{4,3,2,1,0:T(8,128)} copy(f32[2,4,4,64,256]{4,3,0,2,1:T(8,128)S(1)} %convert_bitcast_fusion) | data formatting | bytes 4194304 | tf_op jit(solution)/shard_map/convert_element_type | solution.py:434
  80.2 0.7 copy.12
Async XLA Ops:
  1.4 1.2 %copy-start = (bf16[2,1,1024,256]{3,2,1,0:T(8,128)(2,1)S(1)}, bf16[2,1,1024,256]{3,2,1,0:T(8,128)(2,1)}, u32[]{:S(2)}) copy-start(bf16[2,1,1024,256]{3,2,1,0:T(8,128)(2,1)} %param.6) | copy-start | bytes 3145732
  2.6 1.0 %copy-start.1 = (bf16[2,1,1,128,1024]{4,3,2,1,0:T(8,128)(2,1)S(1)}, bf16[2,1,1,128,1024]{4,3,2,1,0:T(8,128)(2,1)}, u32[]{:S(2)}) copy-start(bf16[2,1,1,128,1024]{4,3,2,1,0:T(8,128)(2,1)} %param.7) | copy-start | bytes 1572868
  3.6 0.9 %copy-start.2 = (bf16[1,1,128,1024]{3,2,1,0:T(8,128)(2,1)S(1)}, bf16[1,1,128,1024]{3,2,1,0:T(8,128)(2,1)}, u32[]{:S(2)}) copy-start(bf16[1,1,128,1024]{3,2,1,0:T(8,128)(2,1)} %param.5) | copy-start | bytes 786436
  4.6 0.7 copy-start.3

commit v2 on v1

--- a/solution.py
+++ b/solution.py
@@ -32,13 +32,17 @@
 
 def kernel(
     cfg,
-    state_ref,
-    weights_ref,
-    upstream_ref,
+    state_hbm,
+    weights_hbm,
+    upstream_hbm,
     span_ref,
     order_ref,
     state_out,
     gathered,
+    state_ref,
+    weights_ref,
+    upstream_ref,
+    load_sem,
     kv,
     queries,
     up_rows,
@@ -101,6 +105,14 @@
     def dp_peer(offset):
         return lax.rem(lane + offset, n_dp)
 
+    loads = [
+        pltpu.make_async_copy(src, dst, load_sem.at[i])
+        for i, (src, dst) in enumerate(
+            [(state_hbm, state_ref), (weights_hbm, weights_ref), (upstream_hbm, upstream_ref)]
+        )
+    ]
+    for load in loads:
+        load.start()
     barrier = pltpu.get_barrier_semaphore()
 
     def greet(axis, who):
@@ -197,9 +209,11 @@
 
     def span_at(t):
         anchor = lax.rem(sec - t + n_pipe * ticks, n_pipe)
-        return lax.rem(span_ref[anchor, 0] + (anchor + t) // n_pipe, 2)
+        return lax.rem(span_ref[anchor] + (anchor + t) // n_pipe, 2)
 
     def begin(t, source):
+        if t == 0:
+            loads[0].wait()
         x = source[...].astype(F32)
         squares = x * x
         sums = [
@@ -207,6 +221,8 @@
         ]
         scale = lax.rsqrt(sum(sums[1:], sums[0]) * (1.0 / feat) + EPS)
         normed = (x * scale).astype(BF16)
+        if t == 0:
+            loads[1].wait()
         projected = dot(normed, weights_ref[span_at(t)])
         raw = projected[:, :hd]
         key_raw[t] = raw
@@ -216,6 +232,8 @@
             pl.semaphore_wait(barrier, n_ctx + n_dp)
         for o in range(1, n_ctx):
             kv_copy(t, o, me, ctx_peer(o)).start()
+        if t == 0:
+            loads[2].wait()
         for h in range(heads):
             part = x[:, h * hd : (h + 1) * hd]
             queries[h * rows : (h + 1) * rows, :] = (
@@ -349,16 +367,27 @@
     gathered[me, lane] = total.astype(BF16)
     for o in range(1, n_ctx):
         ga_copy(o, me, ctx_peer(o)).start()
-    for o in range(1, n_dp):
-        gb_copy(o, me, lane, dp_peer(o)).start()
-    for o in range(1, n_ctx):
-        c = ctx_peer(o)
-        ga_copy(o, c, me).wait_recv()
-        for k in range(1, n_dp):
-            gb_copy(k, c, lane, dp_peer(k)).start()
-    for k in range(1, n_dp):
-        for c in range(n_ctx):
-            gb_copy(k, c, dp_peer(k), lane).wait_recv()
+    near = lane + 1 - 2 * lax.rem(lane, 2)
+    hops = n_dp // 2
+
+    def pair(index):
+        return lax.rem(lane + 2 * index, n_dp)
+
+    order = [ctx_peer(o) for o in range(n_ctx)]
+    for o, c in enumerate(order):
+        if o:
+            ga_copy(o, c, me).wait_recv()
+        for k in range(1, hops):
+            gb_copy(k, c, lane, pair(k)).start()
+        gb_copy(0, c, lane, near).start()
+    for c in order:
+        for k in range(1, hops):
+            gb_copy(k, c, pair(k), lane).wait_recv()
+            gb_copy(hops + k - 1, c, pair(k), near).start()
+    for c in order:
+        gb_copy(0, c, near, lane).wait_recv()
+        for k in range(1, hops):
+            gb_copy(0, c, lax.rem(near + 2 * k, n_dp), lane).wait_recv()
     st_copy(ticks - 1).wait_recv()
 
     for t in range(ticks):
@@ -371,8 +400,9 @@
             gr_copy(t, o, me, peer).wait_send()
     for o in range(1, n_dp):
         ws_copy(o, lane, dp_peer(o)).wait_send()
-        for c in range(n_ctx):
-            gb_copy(o, c, lane, dp_peer(o)).wait_send()
+    for c in range(n_ctx):
+        for k in range(2 * hops - 1):
+            gb_copy(k, c, lane, near).wait_send()
     for o in range(1, n_ctx):
         ga_copy(o, me, ctx_peer(o)).wait_send()
 
@@ -390,6 +420,7 @@
     cfg = (n_pipe, n_ctx, n_dp, ticks, half_len)
     dma = pltpu.SemaphoreType.DMA
     vmem = pl.BlockSpec(memory_space=pltpu.VMEM)
+    hbm = pl.BlockSpec(memory_space=pltpu.HBM)
     smem = pl.BlockSpec(memory_space=pltpu.SMEM)
     new_state, gathered = pl.pallas_call(
         functools.partial(kernel, cfg),
@@ -397,9 +428,13 @@
             jax.ShapeDtypeStruct((rows, feat), BF16),
             jax.ShapeDtypeStruct((n_ctx, n_dp, spans, f_dp, cols), BF16),
         ),
-        in_specs=[vmem, vmem, vmem, smem, smem],
+        in_specs=[hbm, hbm, hbm, smem, smem],
         out_specs=(vmem, vmem),
         scratch_shapes=[
+            pltpu.VMEM((rows, feat), BF16),
+            pltpu.VMEM((spans, feat, cols), BF16),
+            pltpu.VMEM((ticks, rows, feat), BF16),
+            dma((3,)),
             pltpu.VMEM((ticks, n_ctx, rows, cols), BF16),
             pltpu.VMEM((stack, hd), BF16),
             pltpu.VMEM((stack, hd), BF16),
@@ -427,10 +462,10 @@
         + [dma((n_ctx,))] * 2
         + [dma((n_dp, n_ctx)), dma((n_ctx, n_dp))],
         compiler_params=pltpu.CompilerParams(
-            collective_id=0, has_side_effects=True, vmem_limit_bytes=48 * 1024 * 1024
+            collective_id=0, has_side_effects=True, vmem_limit_bytes=60 * 1024 * 1024
         ),
         name="window",
-    )(state[0, 0], weights[:, 0], out_grad[:, 0, 0], start_span, block_order)
+    )(state[0, 0], weights[:, 0], out_grad[:, 0, 0], start_span[:, 0], block_order)
     grads = gathered.transpose(2, 0, 1, 3, 4).reshape(spans, feat, cols).astype(F32)
     return (new_state[None, None], grads[:, None])
 

time: 81.5 us -> 76.6 us (0.940)
  local copies, waits for them, and re-layouts: 6.78 us -> 2.17 us
  Pallas kernels: 73.3 us -> 71.8 us
  other arithmetic: 0.25 us -> 1.47 us
    unnamed x10 -> x3, local copies, waits for them, and re-layouts: 5.31 us -> 0.71 us
    pallas_call x1, Pallas kernels: 73.3 us -> 71.8 us  [shards(): pl.pallas_call(functools.partial(kernel, cfg), out_shape=(jax.ShapeDtypeS...]
    convert_element_type x1, other arithmetic: 0.25 us -> 1.47 us  [shards(): gathered.transpose(2, 0, 1, 3, 4).reshape(spans, feat, cols).astype(F32)]
where the time goes in v2:
time: 76.6 us; the launch traced here: 76 us
  Pallas kernels  71.8 us (94%)
  local copies, waits for them, and re-layouts  2.17 us (3%)
  other arithmetic  1.47 us (2%)
    pallas_call x1, Pallas kernels, shards(): pl.pallas_call(functools.partial(kernel, cfg), out_shape=(jax.ShapeDtypeS...  71.8 us

profile of v2, /device:TPU:17, one launch (start us, length us, event | category | flops | bytes accessed | tf_op | source)
XLA Modules:
  0.0 76.0 jit_solution(6588023204300672330)
XLA Ops:
  0.6 71.8 %window.1 = (bf16[128,1024]{1,0:T(8,128)(2,1)}, bf16[4,4,2,64,256]{4,3,2,1,0:T(8,128)(2,1)}) custom-call(bf16[128,1024]{1,0:T(8,128)(2,1)} %bitcast.13, bf16[2,1024,256]{2,1,0:T(8,128)(2,1)} %bitcast.11, bf16[2,128,1024]{2,1,0:T(8,128)(2,1)} %bitcast.12, s32[2]{0:T(128)} %bitcast.15, s32[8]{0:T(128)} %order_ref.1), custom_call_target="tpu_custom_call" | custom-call | tf_op jit(solution)/shard_map/window/pallas_call | solution.py:425
  72.4 1.5 %convert_bitcast_fusion = f32[2,4,4,64,256]{4,3,0,2,1:T(8,128)S(1)} fusion(bf16[4,4,2,64,256]{4,3,2,1,0:T(8,128)(2,1)} %get-tuple-element.5), kind=kLoop, calls=%fused_computation | loop fusion | flops 524288 | bytes 3145728 | tf_op jit(solution)/shard_map/convert_element_type | solution.py:469
  73.9 0.0 copy-start
  73.9 1.5 %copy.7 = f32[2,4,4,64,256]{4,3,2,1,0:T(8,128)} copy(f32[2,4,4,64,256]{4,3,0,2,1:T(8,128)S(1)} %convert_bitcast_fusion) | data formatting | bytes 4194304 | tf_op jit(solution)/shard_map/convert_element_type | solution.py:469
  75.3 0.0 copy-done
  75.3 0.7 copy.10
Async XLA Ops:
  73.9 1.5 %copy-start = (bf16[128,1024]{1,0:T(8,128)(2,1)S(1)}, bf16[128,1024]{1,0:T(8,128)(2,1)}, u32[]{:S(2)}) copy-start(bf16[128,1024]{1,0:T(8,128)(2,1)} %get-tuple-element.4) | copy-start | bytes 786436

commit v3 on v2

--- a/solution.py
+++ b/solution.py
@@ -113,6 +113,47 @@
     ]
     for load in loads:
         load.start()
+    def beside(side):
+        return lax.rem(me + 2 * side - 1 + n_ctx, n_ctx)
+
+    def exists(side):
+        return me > 0 if side == 0 else me < n_ctx - 1
+
+    def from_line(index, act):
+        distance = index + 1
+
+        @pl.when(me - distance >= 0)
+        def _():
+            act(me - distance, 1)
+
+        @pl.when(me + distance < n_ctx)
+        def _():
+            act(me + distance, 0)
+
+    def spread(copy):
+        for side in (0, 1):
+
+            @pl.when(exists(side))
+            def _(side=side):
+                copy(me, side).start()
+
+    def take(copy, owner, side):
+        copy(owner, side).wait_recv()
+
+        @pl.when(exists(side))
+        def _():
+            copy(owner, side).start()
+
+    def drain(copy):
+        def sent(owner, side):
+            @pl.when(exists(side))
+            def _():
+                copy(owner, side).wait_send()
+
+        for side in (0, 1):
+            sent(me, side)
+        steps(n_ctx - 1, lambda index: from_line(index, sent))
+
     barrier = pltpu.get_barrier_semaphore()
 
     def greet(axis, who):
@@ -135,9 +176,10 @@
             device_id_type=MESH,
         )
 
-    def kv_copy(t, o, owner, to):
+    def kv_copy(t, owner, side):
+        block = kv.at[t, owner]
         return remote(
-            kv.at[t, owner], kv.at[t, owner], kv_send.at[t, o], kv_recv.at[t, owner], "ctx", to
+            block, block, kv_send.at[t, owner, side], kv_recv.at[t, owner], "ctx", beside(side)
         )
 
     def nt_copy(t, o, frm, to):
@@ -160,14 +202,10 @@
             to,
         )
 
-    def gr_copy(t, o, owner, to):
+    def gr_copy(t, owner, side):
+        block = grad_rows.at[t, owner]
         return remote(
-            grad_rows.at[t, owner],
-            grad_rows.at[t, owner],
-            gr_send.at[t, o],
-            gr_recv.at[t, owner],
-            "ctx",
-            to,
+            block, block, gr_send.at[t, owner, side], gr_recv.at[t, owner], "ctx", beside(side)
         )
 
     def st_copy(t):
@@ -177,20 +215,20 @@
     def ws_copy(o, frm, to):
         return remote(wsend.at[to], wrecv.at[frm], ws_send.at[o], ws_recv.at[frm], "dp", to)
 
-    def ga_copy(o, owner, to):
+    def piece(c, d):
+        first = pl.multiple_of((c * n_dp + d) * f_dp, f_dp)
+        return gathered.at[:, pl.ds(first, f_dp), :]
+
+    def ga_copy(owner, side):
+        block = piece(owner, lane)
         return remote(
-            gathered.at[owner, lane],
-            gathered.at[owner, lane],
-            ga_send.at[o],
-            ga_recv.at[owner],
-            "ctx",
-            to,
+            block, block, ga_send.at[owner, side], ga_recv.at[owner], "ctx", beside(side)
         )
 
     def gb_copy(o, c, owner, to):
         return remote(
-            gathered.at[c, owner],
-            gathered.at[c, owner],
+            piece(c, owner),
+            piece(c, owner),
             gb_send.at[o, c],
             gb_recv.at[c, owner],
             "dp",
@@ -230,8 +268,7 @@
         kv[t, me] = jnp.concatenate([key_unit, projected[:, hd:]], axis=1).astype(BF16)
         if t == 0:
             pl.semaphore_wait(barrier, n_ctx + n_dp)
-        for o in range(1, n_ctx):
-            kv_copy(t, o, me, ctx_peer(o)).start()
+        spread(functools.partial(kv_copy, t))
         if t == 0:
             loads[2].wait()
         for h in range(heads):
@@ -243,8 +280,6 @@
             up = upstream_ref[t, :, h * hd : (h + 1) * hd]
             up_rows[h * rows : (h + 1) * rows, :] = up
             up_cols[:, h * rows : (h + 1) * rows] = up.astype(F32).T.astype(BF16)
-        for o in range(1, n_ctx):
-            nt_copy(t, o, me, ctx_peer(o)).start()
 
     def attend(t, block, first):
         keys = kv[t, block, :, :hd]
@@ -305,18 +340,19 @@
         delta = sums[:, :hd]
         back = scale * (delta - unit * jnp.mean(delta * unit, axis=1, keepdims=True))
         grad_rows[t, me] = jnp.concatenate([back, sums[:, hd:]], axis=1).astype(BF16)
-        for o in range(1, n_ctx):
-            gr_copy(t, o, me, ctx_peer(o)).start()
+        spread(functools.partial(gr_copy, t))
 
     def weight_slice(t):
         own = normed_t[t, pl.ds(pl.multiple_of(me * f_ctx, 16), f_ctx), :]
-        total = dot(own, grad_rows[t, me])
+        slices[t] = dot(own, grad_rows[t, me])
         for o in range(1, n_ctx):
-            peer = ctx_peer(o)
-            nt_copy(t, o, peer, me).wait_recv()
-            gr_copy(t, o, peer, me).wait_recv()
-            total = total + dot(normed_in[t, peer], grad_rows[t, peer])
-        return total
+            nt_copy(t, o, ctx_peer(o), me).wait_recv()
+
+        def add(owner, side):
+            take(functools.partial(gr_copy, t), owner, side)
+            slices[t] += dot(normed_in[t, owner], grad_rows[t, owner])
+
+        steps(n_ctx - 1, lambda index: from_line(index, add))
 
     for t in range(ticks):
         if t == 0:
@@ -329,12 +365,13 @@
         if t > 0:
             finish_rows(t - 1)
 
-        def later(index, t=t):
-            peer = ctx_peer(index + 1)
-            kv_copy(t, 0, peer, me).wait_recv()
-            attend(t, peer, False)
-
-        steps(n_ctx - 1, later)
+        def later(owner, side, t=t):
+            take(functools.partial(kv_copy, t), owner, side)
+            attend(t, owner, False)
+
+        steps(n_ctx - 1, lambda index, later=later: from_line(index, later))
+        for o in range(1, n_ctx):
+            nt_copy(t, o, me, ctx_peer(o)).start()
         update(t, source)
 
         def give(index, t=t):
@@ -346,9 +383,9 @@
         term_own[t] = backward(t, me)
 
     for t in range(ticks - 1):
-        slices[t] = weight_slice(t)
+        weight_slice(t)
     finish_rows(ticks - 1)
-    slices[ticks - 1] = weight_slice(ticks - 1)
+    weight_slice(ticks - 1)
     picked = [span_at(t).astype(F32) for t in range(ticks)]
     for d in range(n_dp):
         cut = slice(d * f_dp, (d + 1) * f_dp)
@@ -364,27 +401,33 @@
         peer = dp_peer(o)
         ws_copy(o, peer, lane).wait_recv()
         total = total + wrecv[peer].astype(F32)
-    gathered[me, lane] = total.astype(BF16)
-    for o in range(1, n_ctx):
-        ga_copy(o, me, ctx_peer(o)).start()
+    gathered[:, pl.ds(pl.multiple_of((me * n_dp + lane) * f_dp, f_dp), f_dp), :] = total.astype(BF16)
+    spread(ga_copy)
     near = lane + 1 - 2 * lax.rem(lane, 2)
     hops = n_dp // 2
 
     def pair(index):
         return lax.rem(lane + 2 * index, n_dp)
 
-    order = [ctx_peer(o) for o in range(n_ctx)]
-    for o, c in enumerate(order):
-        if o:
-            ga_copy(o, c, me).wait_recv()
+    def across(c):
         for k in range(1, hops):
             gb_copy(k, c, lane, pair(k)).start()
         gb_copy(0, c, lane, near).start()
-    for c in order:
+
+    def onward(c):
         for k in range(1, hops):
             gb_copy(k, c, pair(k), lane).wait_recv()
             gb_copy(hops + k - 1, c, pair(k), near).start()
-    for c in order:
+
+    def reach(owner, side):
+        take(ga_copy, owner, side)
+        across(owner)
+
+    across(me)
+    steps(n_ctx - 1, lambda index: from_line(index, reach))
+    onward(me)
+    steps(n_ctx - 1, lambda index: from_line(index, lambda owner, side: onward(owner)))
+    for c in range(n_ctx):
         gb_copy(0, c, near, lane).wait_recv()
         for k in range(1, hops):
             gb_copy(0, c, lax.rem(near + 2 * k, n_dp), lane).wait_recv()
@@ -392,19 +435,18 @@
 
     for t in range(ticks):
         st_copy(t).wait_send()
+        drain(functools.partial(kv_copy, t))
+        drain(functools.partial(gr_copy, t))
         for o in range(1, n_ctx):
             peer = ctx_peer(o)
-            kv_copy(t, o, me, peer).wait_send()
             nt_copy(t, o, me, peer).wait_send()
             kt_copy(t, o, me, peer).wait_send()
-            gr_copy(t, o, me, peer).wait_send()
     for o in range(1, n_dp):
         ws_copy(o, lane, dp_peer(o)).wait_send()
     for c in range(n_ctx):
         for k in range(2 * hops - 1):
             gb_copy(k, c, lane, near).wait_send()
-    for o in range(1, n_ctx):
-        ga_copy(o, me, ctx_peer(o)).wait_send()
+    drain(ga_copy)
 
 
 def shards(sizes, state, weights, out_grad, start_span, block_order):
@@ -426,7 +468,7 @@
         functools.partial(kernel, cfg),
         out_shape=(
             jax.ShapeDtypeStruct((rows, feat), BF16),
-            jax.ShapeDtypeStruct((n_ctx, n_dp, spans, f_dp, cols), BF16),
+            jax.ShapeDtypeStruct((spans, feat, cols), BF16),
         ),
         in_specs=[hbm, hbm, hbm, smem, smem],
         out_specs=(vmem, vmem),
@@ -456,18 +498,19 @@
             pltpu.VMEM((n_dp, spans, f_dp, cols), BF16),
             pltpu.VMEM((n_dp, spans, f_dp, cols), BF16),
         ]
-        + [dma((ticks, n_ctx))] * 8
+        + [dma((ticks, n_ctx, 2)), dma((ticks, n_ctx))]
+        + [dma((ticks, n_ctx))] * 4
+        + [dma((ticks, n_ctx, 2)), dma((ticks, n_ctx))]
         + [dma((ticks,))] * 2
         + [dma((n_dp,))] * 2
-        + [dma((n_ctx,))] * 2
+        + [dma((n_ctx, 2)), dma((n_ctx,))]
         + [dma((n_dp, n_ctx)), dma((n_ctx, n_dp))],
         compiler_params=pltpu.CompilerParams(
             collective_id=0, has_side_effects=True, vmem_limit_bytes=60 * 1024 * 1024
         ),
         name="window",
     )(state[0, 0], weights[:, 0], out_grad[:, 0, 0], start_span[:, 0], block_order)
-    grads = gathered.transpose(2, 0, 1, 3, 4).reshape(spans, feat, cols).astype(F32)
-    return (new_state[None, None], grads[:, None])
+    return (new_state[None, None], gathered.astype(F32)[:, None])
 
 
 def solution(mesh):

time: 76.6 us -> 81.7 us (1.067)
  the two profiles are of different devices: /device:TPU:17 before, /device:TPU:3 now
where the time goes in v3:
time: 81.7 us; the launch traced here: 81.5 us
  Pallas kernels  77.4 us (95%)
  other arithmetic  2.75 us (3%)
    pallas_call x1, Pallas kernels, shards(): pl.pallas_call(functools.partial(kernel, cfg), out_shape=(jax.ShapeDtypeS...  77.4 us
    unnamed x1, other arithmetic  2.75 us

profile of v3, /device:TPU:3, one launch (start us, length us, event | category | flops | bytes accessed | tf_op | source)
XLA Modules:
  0.0 81.5 jit_solution(4370081224798168846)
XLA Ops:
  0.6 77.4 %window.1 = (bf16[128,1024]{1,0:T(8,128)(2,1)}, bf16[2,1024,256]{2,1,0:T(8,128)(2,1)}) custom-call(bf16[128,1024]{1,0:T(8,128)(2,1)} %bitcast.13, bf16[2,1024,256]{2,1,0:T(8,128)(2,1)} %bitcast.11, bf16[2,128,1024]{2,1,0:T(8,128)(2,1)} %bitcast.12, s32[2]{0:T(128)} %bitcast.15, s32[8]{0:T(128)} %order_ref.1), custom_call_target="tpu_custom_call" | custom-call | tf_op jit(solution)/shard_map/window/pallas_call | solution.py:467
  78.1 0.0 copy-start
  78.1 2.7 %bitcast_convert_fusion = f32[2,1,1024,256]{3,2,1,0:T(8,128)} fusion(bf16[2,1024,256]{2,1,0:T(8,128)(2,1)} %get-tuple-element.5), kind=kLoop, calls=%fused_computation | loop fusion | flops 524288 | bytes 3145728
  80.8 0.0 copy-done
  80.8 0.7 copy.9
Async XLA Ops:
  78.1 2.8 %copy-start = (bf16[128,1024]{1,0:T(8,128)(2,1)S(1)}, bf16[128,1024]{1,0:T(8,128)(2,1)}, u32[]{:S(2)}) copy-start(bf16[128,1024]{1,0:T(8,128)(2,1)} %get-tuple-element.4) | copy-start | bytes 786436

commit v4 on v2

--- a/solution.py
+++ b/solution.py
@@ -264,15 +264,19 @@
                 totals[:, cut] += total
                 out_cols[:, cut] += mixed
 
-    def update(t, source):
+    def normalise():
         inverse = 1.0 / totals[...]
         totals[...] = inverse
-        power = jnp.zeros((1, rows), F32)
         for h in range(heads):
             cut = slice(h * rows, (h + 1) * rows)
             part = out_cols[:, cut] * inverse[:, cut]
             out_cols[:, cut] = part
             deltas[:, cut] = jnp.sum(part * up_cols[:, cut].astype(F32), axis=0, keepdims=True)
+
+    def update(t, source):
+        power = jnp.zeros((1, rows), F32)
+        for h in range(heads):
+            part = out_cols[:, h * rows : (h + 1) * rows]
             power = power + jnp.sum(part * part, axis=0, keepdims=True)
         scale = lax.rsqrt(power * (1.0 / feat) + EPS)
         for h in range(heads):
@@ -335,7 +339,9 @@
             attend(t, peer, False)
 
         steps(n_ctx - 1, later)
-        update(t, source)
+        normalise()
+        if t < ticks - 1:
+            update(t, source)
 
         def give(index, t=t):
             peer = ctx_peer(index + 1)
@@ -344,6 +350,8 @@
 
         steps(n_ctx - 1, give)
         term_own[t] = backward(t, me)
+        if t == ticks - 1:
+            update(t, source)
 
     for t in range(ticks - 1):
         slices[t] = weight_slice(t)

time: 76.6 us -> 76.2 us (level)
  no operation moved by 1% of the time
where the time goes in v4:
time: 76.2 us; the launch traced here: 76 us
  Pallas kernels  71.8 us (94%)
  local copies, waits for them, and re-layouts  2.17 us (3%)
  other arithmetic  1.47 us (2%)
    pallas_call x1, Pallas kernels, shards(): pl.pallas_call(functools.partial(kernel, cfg), out_shape=(jax.ShapeDtypeS...  71.8 us

profile of v4, /device:TPU:17, one launch (start us, length us, event | category | flops | bytes accessed | tf_op | source)
XLA Modules:
  0.0 76.0 jit_solution(12575721841012563461)
XLA Ops:
  0.6 71.8 %window.1 = (bf16[128,1024]{1,0:T(8,128)(2,1)}, bf16[4,4,2,64,256]{4,3,2,1,0:T(8,128)(2,1)}) custom-call(bf16[128,1024]{1,0:T(8,128)(2,1)} %bitcast.13, bf16[2,1024,256]{2,1,0:T(8,128)(2,1)} %bitcast.11, bf16[2,128,1024]{2,1,0:T(8,128)(2,1)} %bitcast.12, s32[2]{0:T(128)} %bitcast.15, s32[8]{0:T(128)} %order_ref.1), custom_call_target="tpu_custom_call" | custom-call | tf_op jit(solution)/shard_map/window/pallas_call | solution.py:433
  72.4 1.5 %convert_bitcast_fusion = f32[2,4,4,64,256]{4,3,0,2,1:T(8,128)S(1)} fusion(bf16[4,4,2,64,256]{4,3,2,1,0:T(8,128)(2,1)} %get-tuple-element.5), kind=kLoop, calls=%fused_computation | loop fusion | flops 524288 | bytes 3145728 | tf_op jit(solution)/shard_map/convert_element_type | solution.py:477
  73.9 0.0 copy-start
  73.9 1.5 %copy.7 = f32[2,4,4,64,256]{4,3,2,1,0:T(8,128)} copy(f32[2,4,4,64,256]{4,3,0,2,1:T(8,128)S(1)} %convert_bitcast_fusion) | data formatting | bytes 4194304 | tf_op jit(solution)/shard_map/convert_element_type | solution.py:477
  75.3 0.0 copy-done
  75.3 0.7 copy.10
Async XLA Ops:
  73.9 1.5 %copy-start = (bf16[128,1024]{1,0:T(8,128)(2,1)S(1)}, bf16[128,1024]{1,0:T(8,128)(2,1)}, u32[]{:S(2)}) copy-start(bf16[128,1024]{1,0:T(8,128)(2,1)} %get-tuple-element.4) | copy-start | bytes 786436

commit v5 on v4

--- a/solution.py
+++ b/solution.py
@@ -243,8 +243,6 @@
             up = upstream_ref[t, :, h * hd : (h + 1) * hd]
             up_rows[h * rows : (h + 1) * rows, :] = up
             up_cols[:, h * rows : (h + 1) * rows] = up.astype(F32).T.astype(BF16)
-        for o in range(1, n_ctx):
-            nt_copy(t, o, me, ctx_peer(o)).start()
 
     def attend(t, block, first):
         keys = kv[t, block, :, :hd]
@@ -349,6 +347,8 @@
             kt_copy(t, index + 1, me, peer).start()
 
         steps(n_ctx - 1, give)
+        for o in range(1, n_ctx):
+            nt_copy(t, o, me, ctx_peer(o)).start()
         term_own[t] = backward(t, me)
         if t == ticks - 1:
             update(t, source)

time: 76.2 us -> 78.3 us (1.028)
  Pallas kernels: 71.8 us -> 73.4 us
    pallas_call x1, Pallas kernels: 71.8 us -> 73.4 us  [shards(): pl.pallas_call(functools.partial(kernel, cfg), out_shape=(jax.ShapeDtypeS...]
where the time goes in v5:
time: 78.3 us; the launch traced here: 77.7 us
  Pallas kernels  73.4 us (94%)
  local copies, waits for them, and re-layouts  2.17 us (3%)
  other arithmetic  1.47 us (2%)
    pallas_call x1, Pallas kernels, shards(): pl.pallas_call(functools.partial(kernel, cfg), out_shape=(jax.ShapeDtypeS...  73.4 us

profile of v5, /device:TPU:17, one launch (start us, length us, event | category | flops | bytes accessed | tf_op | source)
XLA Modules:
  0.0 77.7 jit_solution(10897403026048486861)
XLA Ops:
  0.6 73.4 %window.1 = (bf16[128,1024]{1,0:T(8,128)(2,1)}, bf16[4,4,2,64,256]{4,3,2,1,0:T(8,128)(2,1)}) custom-call(bf16[128,1024]{1,0:T(8,128)(2,1)} %bitcast.13, bf16[2,1024,256]{2,1,0:T(8,128)(2,1)} %bitcast.11, bf16[2,128,1024]{2,1,0:T(8,128)(2,1)} %bitcast.12, s32[2]{0:T(128)} %bitcast.15, s32[8]{0:T(128)} %order_ref.1), custom_call_target="tpu_custom_call" | custom-call | tf_op jit(solution)/shard_map/window/pallas_call | solution.py:433
  74.0 1.5 %convert_bitcast_fusion = f32[2,4,4,64,256]{4,3,0,2,1:T(8,128)S(1)} fusion(bf16[4,4,2,64,256]{4,3,2,1,0:T(8,128)(2,1)} %get-tuple-element.5), kind=kLoop, calls=%fused_computation | loop fusion | flops 524288 | bytes 3145728 | tf_op jit(solution)/shard_map/convert_element_type | solution.py:477
  75.5 0.0 copy-start
  75.5 1.5 %copy.7 = f32[2,4,4,64,256]{4,3,2,1,0:T(8,128)} copy(f32[2,4,4,64,256]{4,3,0,2,1:T(8,128)S(1)} %convert_bitcast_fusion) | data formatting | bytes 4194304 | tf_op jit(solution)/shard_map/convert_element_type | solution.py:477
  76.9 0.0 copy-done
  76.9 0.7 copy.10
Async XLA Ops:
  75.5 1.5 %copy-start = (bf16[128,1024]{1,0:T(8,128)(2,1)S(1)}, bf16[128,1024]{1,0:T(8,128)(2,1)}, u32[]{:S(2)}) copy-start(bf16[128,1024]{1,0:T(8,128)(2,1)} %get-tuple-element.4) | copy-start | bytes 786436
